TPU v7x, 1024 devices: a whole 4x8x16 slice. The times are simulated.
1024 devices in a mesh: leaf: 64 (over y_hi, z, core), grp: 16 (over y_lo, x).
Axes of the slice: x: 4, y: 8 (y_hi: 2, y_lo: 4; y = y_hi * 4 + y_lo), z: 16, core: 2. Of those that a mesh axis runs over, the one named last changes fastest.
Arguments:
- charges: bfloat16 [32768, 16, 128], P(('leaf', 'grp')), may hold values from -6 to 6
- points: bfloat16 [32768, 3, 128], P(('leaf', 'grp')), may hold values from 0 to 13
- near_list: int32 [32768, 20], P(('leaf', 'grp')), may hold values from 0 to 32767, as said below
- near_count: int32 [32768], P(('leaf', 'grp')), may hold values from 1 to 20
- basis: bfloat16 [32768, 64, 128], P(('leaf', 'grp')), may hold values from -0.5 to 0.5
- far_list: int32 [32768, 6], P(('leaf', 'grp')), may hold values from 0 to 32767, as said below
- leaf_coupling_stack: bfloat16 [32768, 64, 384], P(('leaf', 'grp')), may hold values from -0.3125 to 0.3125
- transfer: bfloat16 [1024, 64, 2048], P(('leaf', 'grp')), may hold values from -0.375 to 0.375
- node_list: int32 [1024, 2], P(('leaf', 'grp')), may hold values from 0 to 15, as said below
- node_coupling: bfloat16 [1024, 64, 128], P(('leaf', 'grp')), may hold values from -0.5 to 0.5
- lift: bfloat16 [64, 16, 64, 64], P('leaf'), may hold values from -0.375 to 0.375
- top_list: int32 [64, 4], P('leaf'), may hold values from 0 to 63, as said below
- top_coupling: bfloat16 [64, 64, 256], P('leaf'), may hold values from -0.375 to 0.375
Outputs:
- potentials: bfloat16 [32768, 16, 128], P(('leaf', 'grp'))
Inputs may be any that keep to these rules, and one draw needn't show every extreme that they name: `near_list`: row t lists leaf t first, then 20 - 1 distinct other leaves whose cyclic distance to t in tree order is 1 to 12. `far_list`: row t lists 6 distinct leaves whose cyclic distance to t in tree order is 13 to 20. `node_list`: row n lists distinct indices within node n's group, never n mod 16 itself. `top_list`: row g lists distinct groups other than g.
All inputs are finite; a program needn't handle non-finite values.
Results may differ from a plain program's by a relative error of at most 0.015.
Values may be sent and summed in bfloat16 or wider, within the bound.
A program may use at most 32 MiB of HBM per device.

v0:
```python
import jax
import jax.numpy as jnp
from jax import lax
from jax.sharding import PartitionSpec as P

NEAR_REACH = 12
FAR_REACH = 20


def extended(x, sides, width):
    for axis, dim in sides:
        count, length = (lax.axis_size(axis), x.shape[dim])
        up = [(i, (i + 1) % count) for i in range(count)]
        down = [(j, i) for i, j in up]
        last = lax.slice_in_dim(x, length - width, length, axis=dim)
        first = lax.slice_in_dim(x, 0, width, axis=dim)
        before = lax.ppermute(last, axis, up)
        after = lax.ppermute(first, axis, down)
        x = jnp.concatenate([before, x, after], axis=dim)
    return x


def near_kernel(leaf_cluster_index, block_list, block_live, target_pts, source_pts, leaf_total):
    leaf_gap = (
        jnp.mod(leaf_cluster_index[:, None] - block_list + leaf_total // 2, leaf_total)
        - leaf_total // 2
    )
    leaf_gap = leaf_gap.astype(jnp.float32)
    target_f = target_pts.astype(jnp.float32)
    source_f = source_pts.astype(jnp.float32)
    across = float(NEAR_REACH)
    gap_x = leaf_gap[:, :, None, None] + target_f[:, None, 0, :, None] - source_f[:, :, 0, None, :]
    gap_y = across * (target_f[:, None, 1, :, None] - source_f[:, :, 1, None, :])
    gap_z = across * (target_f[:, None, 2, :, None] - source_f[:, :, 2, None, :])
    squared = gap_x * gap_x + gap_y * gap_y + gap_z * gap_z + 0.25
    slot_ids = jnp.arange(block_list.shape[1], dtype=jnp.int32)
    live_mask = (slot_ids[None, :] < block_live[:, None]).astype(jnp.float32)
    kernel = lax.rsqrt(squared * float(target_pts.shape[-1])) * live_mask[:, :, None, None]
    return kernel.astype(jnp.bfloat16)


def shards(
    charges,
    points,
    near_list,
    near_count,
    basis,
    far_list,
    leaf_coupling_stack,
    transfer,
    node_list,
    node_coupling,
    lift,
    top_list,
    top_coupling,
):
    leaves_here = charges.shape[0]
    right_sides = charges.shape[1]
    leaf_pts = charges.shape[2]
    rank_size = basis.shape[1]
    far_rim = FAR_REACH
    leaf_total = leaves_here * lax.axis_size(("leaf", "grp"))
    first_leaf = lax.axis_index(("leaf", "grp")) * leaves_here
    multipole_moments = jnp.einsum(
        "trp,tkp->trk", charges, basis, preferred_element_type=jnp.float32
    ).astype(jnp.bfloat16)
    flat_charges = charges.reshape(leaves_here, right_sides * leaf_pts)
    flat_points = points.reshape(leaves_here, 3 * leaf_pts)
    flat_moments = multipole_moments.reshape(leaves_here, right_sides * rank_size)
    charge_end = right_sides * leaf_pts
    point_end = charge_end + 3 * leaf_pts
    near_offset = FAR_REACH
    widened = extended(
        jnp.concatenate([flat_charges, flat_points, flat_moments], 1),
        ((("leaf", "grp"), 0),),
        far_rim,
    )
    ext_charges = widened[:, :charge_end]
    ext_points = widened[:, charge_end:point_end]
    ext_moments = widened[:, point_end:]
    near_extended = leaves_here + 2 * near_offset
    far_extended = leaves_here + 2 * far_rim
    ext_charges = ext_charges.reshape(near_extended, right_sides, leaf_pts)
    ext_points = ext_points.reshape(near_extended, 3, leaf_pts)
    ext_moments = ext_moments.reshape(far_extended, right_sides, rank_size)
    leaf_cluster_index = first_leaf + jnp.arange(leaves_here, dtype=jnp.int32)
    near_slot = jnp.mod(near_list - first_leaf + near_offset, leaf_total)
    far_slot = jnp.mod(far_list - first_leaf + far_rim, leaf_total)
    block_total = leaves_here // 4
    near_width = near_list.shape[1]

    def near_block(inputs_block):
        block_ids, block_list, block_slot, block_live, block_points = inputs_block
        kernel = near_kernel(
            block_ids, block_list, block_live, block_points, ext_points[block_slot], leaf_total
        )
        return jnp.einsum(
            "tjip,tjrp->tri", kernel, ext_charges[block_slot], preferred_element_type=jnp.float32
        )

    near_part = lax.map(
        near_block,
        (
            leaf_cluster_index.reshape(block_total, 4),
            near_list.reshape(block_total, 4, near_width),
            near_slot.reshape(block_total, 4, near_width),
            near_count.reshape(block_total, 4),
            points.reshape(block_total, 4, 3, leaf_pts),
        ),
    )
    near_part = near_part.reshape(leaves_here, right_sides, leaf_pts)
    far_count = far_list.shape[1]
    coupled = jnp.einsum(
        "tjrq,tkjq->trk",
        ext_moments[far_slot],
        leaf_coupling_stack.reshape(leaves_here, rank_size, far_count, rank_size),
        preferred_element_type=jnp.float32,
    )
    self_transfer_matrix = transfer[0].reshape(rank_size, leaves_here, rank_size)
    node_moment = jnp.einsum(
        "dnw,edw->ne", multipole_moments, self_transfer_matrix, preferred_element_type=jnp.float32
    ).astype(jnp.bfloat16)
    group_moments = lax.all_gather(node_moment[None], "grp", axis=0, tiled=True)
    node_sources = node_list.shape[1]
    group_local = jnp.einsum(
        "jrq,kjq->rk",
        group_moments[node_list[0]],
        node_coupling[0].reshape(rank_size, node_sources, rank_size),
        preferred_element_type=jnp.float32,
    )
    own_lift = lax.dynamic_index_in_dim(lift[0], lax.axis_index("grp"), 0, keepdims=False)
    own_term = jnp.einsum("rq,kq->rk", node_moment, own_lift, preferred_element_type=jnp.float32)
    top_moment = lax.psum(own_term, "grp").astype(jnp.bfloat16)
    top_moments = lax.all_gather(top_moment[None], "leaf", axis=0, tiled=True)
    top_sources = top_list.shape[1]
    top_local = jnp.einsum(
        "jrq,kjq->rk",
        top_moments[top_list[0]],
        top_coupling[0].reshape(rank_size, top_sources, rank_size),
        preferred_element_type=jnp.float32,
    ).astype(jnp.bfloat16)
    lifted = jnp.einsum("rk,kq->rq", top_local, own_lift, preferred_element_type=jnp.float32)
    resident_node_rows = (lifted + group_local).astype(jnp.bfloat16)
    broadcast_expansion = jnp.einsum(
        "eo,oxa->xea", resident_node_rows, self_transfer_matrix, preferred_element_type=jnp.float32
    )
    leaf_local = (broadcast_expansion + coupled).astype(jnp.bfloat16)
    far_part = jnp.einsum("trk,tkp->trp", leaf_local, basis, preferred_element_type=jnp.float32)
    return (near_part + far_part).astype(jnp.bfloat16)


def solution(mesh):
    return jax.shard_map(
        shards,
        mesh=mesh,
        in_specs=(
            P(("leaf", "grp"), None, None),
            P(("leaf", "grp"), None, None),
            P(("leaf", "grp"), None),
            P(("leaf", "grp")),
            P(("leaf", "grp"), None, None),
            P(("leaf", "grp"), None),
            P(("leaf", "grp"), None, None),
            P(("leaf", "grp"), None, None),
            P(("leaf", "grp"), None),
            P(("leaf", "grp"), None, None),
            P("leaf", None, None, None),
            P("leaf", None),
            P("leaf", None, None),
        ),
        out_specs=P(("leaf", "grp"), None, None),
        check_vma=False,
    )
```

profile of v0, /device:TPU:2, one launch (start us, length us, event | category | flops | bytes accessed | tf_op | source)
XLA Modules:
  0.0 283.0 jit_solution(14145616150512175250)
XLA Ops:
  0.0 1.1 bitcast_dynamic-update-slice_fusion
  1.1 1.3 convolution_convert_fusion
  4.1 15.1 %collective-permute-start.1 = (bf16[20,3456]{1,0:T(8,128)(2,1)}, bf16[20,3456]{1,0:T(8,128)(2,1)S(1)}, u32[]{:S(2)}, u32[]{:S(2)}) collective-permute-start(bf16[20,3456]{1,0:T(8,128)(2,1)} %get-tuple-element.159), channel_id=1, source_target_pairs={{1,0},{2,1},{3,2},{4,3},{5,4},{6,5},{7,6},{8,7},{9,8},{10,9},{11,1... | collective-permute-start | bytes 414728 | tf_op jit(solution)/shard_map/ppermute | solution.py:18
  19.2 1.9 collective-permute-start
  23.3 1.5 reshape_squeeze.9
  25.1 0.8 fusion.26
  25.9 46.5 %psum.7 = bf16[16,64]{1,0:T(8,128)(2,1)S(1)} all-reduce(f32[16,64]{1,0:T(8,128)S(1)} %fusion.26), channel_id=1, replica_groups=mesh['leaf'=64,'grp'=16] {'grp'}, use_global_device_ids=true, to_apply=%region_2.3 | all-reduce | flops 1024 | bytes 6144 | tf_op jit(solution)/shard_map/psum | solution.py:133
  72.4 94.8 %all-gather = bf16[1024,64]{1,0:T(8,128)(2,1)S(1)} all-gather(bf16[16,64]{1,0:T(8,128)(2,1)S(1)} %psum.7), channel_id=2, replica_groups=mesh['leaf'=64,'grp'=16] {'leaf'}, dimensions={0}, use_global_device_ids=true | all-gather | bytes 133120 | tf_op jit(solution)/shard_map/all_gather | solution.py:134
  167.8 0.9 copy.34
  169.9 1.6 fusion.21
  173.7 2.9 %copy.36 = bf16[32,64,384]{1,2,0:T(8,128)(2,1)} copy(bf16[32,64,384]{2,1,0:T(8,128)(2,1)S(1)} %copy-done.1) | data formatting | bytes 3145728 | tf_op jit(solution)/shard_map/reshape | solution.py:116
  176.7 43.0 %all-gather.1 = bf16[256,64]{1,0:T(8,128)(2,1)S(1)} all-gather(bf16[16,64]{1,0:T(8,128)(2,1)S(1)} %fusion.17), channel_id=3, replica_groups=mesh['leaf'=64,'grp'=16] {'grp'}, dimensions={0}, use_global_device_ids=true | all-gather | bytes 34816 | tf_op jit(solution)/shard_map/all_gather | solution.py:123
  220.7 57.6 %while.12 = (s32[]{:T(128)}, f32[8,4,16,128]{3,2,1,0:T(8,128)S(1)}, s32[8,4,20]{2,1,0:T(4,128)}, bf16[72,16,128]{2,1,0:T(8,128)(2,1)S(1)}, s32[8,4]{1,0:T(8,128)...) while((s32[]{:T(128)}, f32[8,4,16,128]{3,2,1,0:T(8,128)S(1)}, ...), condition=%wide.region_1.2_spmd, body=%wide.region_0.1_spmd.sunk | while | flops 60307520 | bytes 2151073 | solution.py:101
  224.6 3.3 %fusion.63 = f32[8,4,16,128]{3,2,1,0:T(8,128)S(1)} fusion(f32[8,4,16,128]{3,2,1,0:T(8,128)S(1)} %get-tuple-element.246, s32[]{:T(128)S(6)} %copy.70, bf16[4,20,16,128]{3,2,1,0:T(8,128)(2,1)S(1)} %bitcast.146, f32[4,20]{1,0:T(4,128)S(1)} %fusion.60, f32[4,20,128]{2,1,0:T(8,128)S(1)} %copy.61, f32[4,128]{1,0:T(4,128)S(1)} %get-tuple-element.229, ...), kind=kOutput, calls=%fused_computation.8.clone.1 | convolution fusion | flops 60293120 | bytes 563204 | tf_op jit(solution)/shard_map/while/body/eval_jaxpr/tjip,tjrp->tri/dot_general | solution.py:97
  231.8 3.3 %fusion.63 = f32[8,4,16,128]{3,2,1,0:T(8,128)S(1)} fusion(f32[8,4,16,128]{3,2,1,0:T(8,128)S(1)} %get-tuple-element.246, s32[]{:T(128)S(6)} %copy.70, bf16[4,20,16,128]{3,2,1,0:T(8,128)(2,1)S(1)} %bitcast.146, f32[4,20]{1,0:T(4,128)S(1)} %fusion.60, f32[4,20,128]{2,1,0:T(8,128)S(1)} %copy.61, f32[4,128]{1,0:T(4,128)S(1)} %get-tuple-element.229, ...), kind=kOutput, calls=%fused_computation.8.clone.1 | convolution fusion | flops 60293120 | bytes 563204 | tf_op jit(solution)/shard_map/while/body/eval_jaxpr/tjip,tjrp->tri/dot_general | solution.py:97
  239.0 3.3 %fusion.63 = f32[8,4,16,128]{3,2,1,0:T(8,128)S(1)} fusion(f32[8,4,16,128]{3,2,1,0:T(8,128)S(1)} %get-tuple-element.246, s32[]{:T(128)S(6)} %copy.70, bf16[4,20,16,128]{3,2,1,0:T(8,128)(2,1)S(1)} %bitcast.146, f32[4,20]{1,0:T(4,128)S(1)} %fusion.60, f32[4,20,128]{2,1,0:T(8,128)S(1)} %copy.61, f32[4,128]{1,0:T(4,128)S(1)} %get-tuple-element.229, ...), kind=kOutput, calls=%fused_computation.8.clone.1 | convolution fusion | flops 60293120 | bytes 563204 | tf_op jit(solution)/shard_map/while/body/eval_jaxpr/tjip,tjrp->tri/dot_general | solution.py:97
  246.2 3.3 %fusion.63 = f32[8,4,16,128]{3,2,1,0:T(8,128)S(1)} fusion(f32[8,4,16,128]{3,2,1,0:T(8,128)S(1)} %get-tuple-element.246, s32[]{:T(128)S(6)} %copy.70, bf16[4,20,16,128]{3,2,1,0:T(8,128)(2,1)S(1)} %bitcast.146, f32[4,20]{1,0:T(4,128)S(1)} %fusion.60, f32[4,20,128]{2,1,0:T(8,128)S(1)} %copy.61, f32[4,128]{1,0:T(4,128)S(1)} %get-tuple-element.229, ...), kind=kOutput, calls=%fused_computation.8.clone.1 | convolution fusion | flops 60293120 | bytes 563204 | tf_op jit(solution)/shard_map/while/body/eval_jaxpr/tjip,tjrp->tri/dot_general | solution.py:97
  253.4 3.3 %fusion.63 = f32[8,4,16,128]{3,2,1,0:T(8,128)S(1)} fusion(f32[8,4,16,128]{3,2,1,0:T(8,128)S(1)} %get-tuple-element.246, s32[]{:T(128)S(6)} %copy.70, bf16[4,20,16,128]{3,2,1,0:T(8,128)(2,1)S(1)} %bitcast.146, f32[4,20]{1,0:T(4,128)S(1)} %fusion.60, f32[4,20,128]{2,1,0:T(8,128)S(1)} %copy.61, f32[4,128]{1,0:T(4,128)S(1)} %get-tuple-element.229, ...), kind=kOutput, calls=%fused_computation.8.clone.1 | convolution fusion | flops 60293120 | bytes 563204 | tf_op jit(solution)/shard_map/while/body/eval_jaxpr/tjip,tjrp->tri/dot_general | solution.py:97
  260.6 3.3 %fusion.63 = f32[8,4,16,128]{3,2,1,0:T(8,128)S(1)} fusion(f32[8,4,16,128]{3,2,1,0:T(8,128)S(1)} %get-tuple-element.246, s32[]{:T(128)S(6)} %copy.70, bf16[4,20,16,128]{3,2,1,0:T(8,128)(2,1)S(1)} %bitcast.146, f32[4,20]{1,0:T(4,128)S(1)} %fusion.60, f32[4,20,128]{2,1,0:T(8,128)S(1)} %copy.61, f32[4,128]{1,0:T(4,128)S(1)} %get-tuple-element.229, ...), kind=kOutput, calls=%fused_computation.8.clone.1 | convolution fusion | flops 60293120 | bytes 563204 | tf_op jit(solution)/shard_map/while/body/eval_jaxpr/tjip,tjrp->tri/dot_general | solution.py:97
  267.8 3.3 %fusion.63 = f32[8,4,16,128]{3,2,1,0:T(8,128)S(1)} fusion(f32[8,4,16,128]{3,2,1,0:T(8,128)S(1)} %get-tuple-element.246, s32[]{:T(128)S(6)} %copy.70, bf16[4,20,16,128]{3,2,1,0:T(8,128)(2,1)S(1)} %bitcast.146, f32[4,20]{1,0:T(4,128)S(1)} %fusion.60, f32[4,20,128]{2,1,0:T(8,128)S(1)} %copy.61, f32[4,128]{1,0:T(4,128)S(1)} %get-tuple-element.229, ...), kind=kOutput, calls=%fused_computation.8.clone.1 | convolution fusion | flops 60293120 | bytes 563204 | tf_op jit(solution)/shard_map/while/body/eval_jaxpr/tjip,tjrp->tri/dot_general | solution.py:97
  275.0 3.3 %fusion.63 = f32[8,4,16,128]{3,2,1,0:T(8,128)S(1)} fusion(f32[8,4,16,128]{3,2,1,0:T(8,128)S(1)} %get-tuple-element.246, s32[]{:T(128)S(6)} %copy.70, bf16[4,20,16,128]{3,2,1,0:T(8,128)(2,1)S(1)} %bitcast.146, f32[4,20]{1,0:T(4,128)S(1)} %fusion.60, f32[4,20,128]{2,1,0:T(8,128)S(1)} %copy.61, f32[4,128]{1,0:T(4,128)S(1)} %get-tuple-element.229, ...), kind=kOutput, calls=%fused_computation.8.clone.1 | convolution fusion | flops 60293120 | bytes 563204 | tf_op jit(solution)/shard_map/while/body/eval_jaxpr/tjip,tjrp->tri/dot_general | solution.py:97
  278.5 0.8 gather_fusion.4
  279.3 2.6 convolution_bitcast_fusion.1
  281.9 1.1 fusion.15
  (182 shorter events, 40.5 us)
Async XLA Ops:
  0.0 1.1 copy-start
  0.0 172.2 %copy-start.2 = (s32[32,20]{0,1:T(8,128)S(1)}, s32[32,20]{0,1:T(8,128)}, u32[]{:S(2)}) copy-start(s32[32,20]{0,1:T(8,128)} %param.17) | copy-start | bytes 7684
  0.0 167.2 %copy-start.5 = (s32[1,4]{1,0:T(1,128)S(1)}, s32[1,4]{1,0:T(1,128)}, u32[]{:S(2)}) copy-start(s32[1,4]{1,0:T(1,128)} %param.26) | copy-start | bytes 52
  0.0 168.7 %copy-start.6 = (s32[1,2]{1,0:T(1,128)S(1)}, s32[1,2]{1,0:T(1,128)}, u32[]{:S(2)}) copy-start(s32[1,2]{1,0:T(1,128)} %param.23) | copy-start | bytes 28
  0.0 173.7 %copy-start.1 = (bf16[32,64,384]{2,1,0:T(8,128)(2,1)S(1)}, bf16[32,64,384]{2,1,0:T(8,128)(2,1)}, u32[]{:S(2)}) copy-start(bf16[32,64,384]{2,1,0:T(8,128)(2,1)} %param.21) | copy-start | bytes 4718596
  4.1 216.4 %collective-permute-start.1 = (bf16[20,3456]{1,0:T(8,128)(2,1)}, bf16[20,3456]{1,0:T(8,128)(2,1)S(1)}, u32[]{:S(2)}, u32[]{:S(2)}) collective-permute-start(bf16[20,3456]{1,0:T(8,128)(2,1)} %get-tuple-element.159), channel_id=1, source_target_pairs={{1,0},{2,1},{3,2},{4,3},{5,4},{6,5},{7,6},{8,7},{9,8},{10,9},{11,1... | collective-permute-start | bytes 414728 | tf_op jit(solution)/shard_map/ppermute | solution.py:18
  19.2 201.3 %collective-permute-start = (bf16[20,3456]{1,0:T(8,128)(2,1)}, bf16[20,3456]{1,0:T(8,128)(2,1)S(1)}, u32[]{:S(2)}, u32[]{:S(2)}) collective-permute-start(bf16[20,3456]{1,0:T(8,128)(2,1)} %get-tuple-element.158), channel_id=1, source_target_pairs={{0,1},{1,2},{2,3},{3,4},{4,5},{5,6},{6,7},{7,8},{8,9},{9,10},{10,1... | collective-permute-start | bytes 414728 | tf_op jit(solution)/shard_map/ppermute | solution.py:17
  171.5 5.1 %copy-start.4 = (bf16[1,64,128]{2,1,0:T(8,128)(2,1)S(1)}, bf16[1,64,128]{2,1,0:T(8,128)(2,1)}, u32[]{:S(2)}) copy-start(bf16[1,64,128]{2,1,0:T(8,128)(2,1)} %param.24) | copy-start | bytes 49156
  171.5 48.7 %copy-start.3 = (f32[16,64]{1,0:T(8,128)S(1)}, f32[16,64]{1,0:T(8,128)}, u32[]{:S(2)}) copy-start(f32[16,64]{1,0:T(8,128)} %fusion.21) | copy-start | bytes 12292
where the time goes:
time: 284 us; the launch traced here: 283 us
  blocking collectives  184 us (65%)
  matrix products  34 us (12%)
  local copies, waits for them, and re-layouts  30.1 us (11%)
  other arithmetic  17.1 us (6%)
  starting transfers between devices  17 us (6%)
    all_gather x1, blocking collectives, shards(): top_moments = lax.all_gather(top_moment[None], 'leaf', axis=0, tiled=True)  94.8 us
    psum x1, blocking collectives, shards(): top_moment = lax.psum(own_term, 'grp').astype(jnp.bfloat16)  46.5 us
    all_gather x1, blocking collectives, shards(): group_moments = lax.all_gather(node_moment[None], 'grp', axis=0, tiled=True)  43 us
    dot_general x8, matrix products, near_block(): jnp.einsum('tjip,tjrp->tri', kernel, ext_charges[block_slot], preferred_e...  26.1 us
    ppermute x1, starting transfers between devices, extended(): after = lax.ppermute(first, axis, down)  15.1 us
  transfers between devices with their start and end apart: 2, of which 0 were waited for; matrix products, arithmetic and copies ran while one was open for 5% of the time, Pallas kernels for 0%

commit v1 on v0

v1 whole, which is shorter than its diff:
```python
import functools

import jax
import jax.numpy as jnp
from jax import lax
from jax.experimental import pallas as pl
from jax.experimental.pallas import tpu as pltpu
from jax.sharding import PartitionSpec as P

NEAR = 12
FAR = 20
EARLY = 6
BF = jnp.bfloat16
F = jnp.float32
MESH = pl.DeviceIdType.MESH
CONTRACT_LAST = (((1,), (1,)), ((), ()))


def dot_t(a, b):
    return lax.dot_general(a, b, CONTRACT_LAST, preferred_element_type=F)


def twice(x):
    return jnp.concatenate([x, x], axis=1)


def kernel(
    total, near_list, near_count, far_list, node_list, top_list,
    charges, points, basis, coupling, transfer, node_coupling, lift, top_coupling,
    out,
    ext_ch, ext_pt, ext_mo, fine, src_ch, rows, tiles, near_acc, spread, coupled,
    basis_v, coupling_v, transfer_v, ncoup_v, lift_v, tcoup_v, group_nm, top_own, top_all, top_part,
    load_sem, halo_send, halo_recv, nm_send, nm_recv, tm_send, tm_recv, tl_send, tl_recv,
):
    leaves = charges.shape[0]
    slots = near_list.shape[0]
    members = group_nm.shape[0]
    quarter, kinds = top_all.shape[0], top_part.shape[0]
    groups = quarter * kinds
    share = groups // members
    rank = ext_mo.shape[2] // 2
    g = lax.axis_index("leaf")
    e = lax.axis_index("grp")
    first = (g * members + e) * leaves
    right = (lax.rem(g + (e + 1) // members, groups), lax.rem(e + 1, members))
    left = (
        lax.rem(g + groups - 1 + (e + members - 1) // members, groups),
        lax.rem(e + members - 1, members),
    )
    kind = lax.rem(e, kinds)
    own_kind = lax.rem(g, kinds)
    catcher = (g // quarter) * kinds
    is_catcher = e // kinds == g // quarter
    target_member = (e // kinds) * kinds + own_kind

    loads = [
        pltpu.make_async_copy(src, dst, load_sem.at[i])
        for i, (src, dst) in enumerate(
            [
                (charges, ext_ch.at[pl.ds(NEAR, leaves)]),
                (basis, basis_v),
                (transfer, transfer_v),
                (lift, lift_v),
                (coupling, coupling_v),
                (node_coupling, ncoup_v),
                (top_coupling, tcoup_v),
            ]
        )
    ]
    for load in loads[:3]:
        load.start()

    barrier = pltpu.get_barrier_semaphore()

    def greet(device):
        pl.semaphore_signal(barrier, inc=1, device_id=device, device_id_type=MESH)

    @pl.when(is_catcher)
    def _():
        def greet_group(i, carry):
            peer = i * kinds + kind

            @pl.when(peer != g)
            def _():
                greet((peer, g // share))

            return carry

        lax.fori_loop(0, quarter, greet_group, 0)

    greet(right)
    greet(left)

    def greet_member(i, carry):
        greet((g, lax.rem(e + i, members)))
        return carry

    lax.fori_loop(1, members, greet_member, 0)
    for load in loads[3:]:
        load.start()

    loads[0].wait()
    loads[1].wait()

    def moment(t, carry):
        b = basis_v[t]
        m = dot_t(ext_ch[NEAR + t], jnp.concatenate([b, b], 0))
        ext_mo[FAR + t] = m.astype(BF)
        return carry

    lax.fori_loop(0, leaves, moment, 0, unroll=8)
    lane = lax.broadcasted_iota(jnp.int32, (ext_mo.shape[1], ext_mo.shape[2]), 1)
    low = lane < rank

    def pair(a, b):
        return jnp.where(low, a, b)

    loads[2].wait()
    packed = [pair(ext_mo[FAR + 2 * u], ext_mo[FAR + 2 * u + 1]) for u in range(leaves // 2)]
    own_nm = dot_t(jnp.concatenate(packed, 1), transfer_v[0])
    group_nm[e] = twice(own_nm).astype(BF)

    fine[...] = points[...].astype(F)
    pad = jnp.zeros((13, points.shape[2]), F)

    def own_points(t, carry):
        p = jnp.concatenate([fine[c, pl.ds(t, 1), :] for c in range(3)] + [pad], 0)
        ext_pt[NEAR + t] = p.astype(BF)
        return carry

    lax.fori_loop(0, leaves, own_points, 0, unroll=4)

    def own_tiles(t, carry):
        cols = ext_pt[NEAR + t].astype(F)[:8].T
        for c in range(3):
            tiles[t, c] = jnp.broadcast_to(cols[:, c : c + 1], tiles.shape[2:]).astype(BF)
        return carry

    def sources(s, carry):
        p = ext_pt[s].astype(F)
        for c in range(3):
            rows[s, c] = jnp.broadcast_to(p[c : c + 1], p.shape).astype(BF)
        src_ch[s] = ext_ch[s]
        return carry

    def no_source(s, carry):
        src_ch[s] = jnp.zeros_like(src_ch[s])
        rows[s] = jnp.zeros_like(rows[s])
        return carry

    scale = F(1.0 / (NEAR * points.shape[2] ** 0.5))
    inverse = BF(1.0 / NEAR**2)
    soft = BF(0.25 / NEAR**2)
    copies = tiles.shape[2] // rows.shape[2]

    def tall(row):
        return jnp.concatenate([row] * copies, 0)

    def near(t, carry):
        acc = jnp.zeros(near_acc.shape[1:], F)
        count = near_count[t]
        for j0 in range(0, slots, 2):
            ks = []
            cs = []
            for j in (j0, j0 + 1):
                s = lax.rem(near_list[j, t] - first + NEAR + total, total)
                s = jnp.clip(s, 0, rows.shape[0] - 1)
                gap = (t + NEAR - s).astype(F).astype(BF)
                dx = tiles[t, 0] - tall(rows[s, 0] - gap)
                dy = tiles[t, 1] - tall(rows[s, 1])
                dz = tiles[t, 2] - tall(rows[s, 2])
                square = dx * dx * inverse + soft + (dy * dy + dz * dz)
                ks.append(lax.rsqrt(square))
                live = jnp.where(j < count, F(1), F(0)).astype(BF)
                cs.append(src_ch[s] * live)
            acc = acc + dot_t(jnp.concatenate(cs, 1), jnp.concatenate(ks, 1))
        near_acc[t] = acc * scale
        return carry

    def near_inner():
        lax.fori_loop(0, leaves, own_tiles, 0, unroll=2)
        lax.fori_loop(0, NEAR, no_source, 0, unroll=4)
        lax.fori_loop(NEAR + leaves, leaves + 2 * NEAR, no_source, 0, unroll=4)
        lax.fori_loop(NEAR, NEAR + leaves, sources, 0, unroll=4)
        lax.fori_loop(NEAR, leaves - NEAR, near, 0, unroll=2)

    ahead = lax.rem(g, groups // 2) < groups // EARLY
    pl.when(ahead)(near_inner)

    begin = e * share
    mine = jnp.logical_and(g >= begin, g < begin + share)
    targets = jnp.where(mine, share - 1, share)
    pl.semaphore_wait(barrier, 2 + (members - 1) + targets)

    def nm_copy(i):
        peer = lax.rem(e + i, members)
        return pltpu.make_async_remote_copy(
            src_ref=group_nm.at[e],
            dst_ref=group_nm.at[e],
            send_sem=nm_send.at[peer],
            recv_sem=nm_recv.at[e],
            device_id=(g, peer),
            device_id_type=MESH,
        )

    def nm_start(i, carry):
        nm_copy(i).start()
        return carry

    lax.fori_loop(1, members, nm_start, 0)

    to_right = []
    to_left = []
    for i, (buf, width) in enumerate([(ext_ch, NEAR), (ext_pt, NEAR), (ext_mo, FAR)]):
        to_right.append(
            pltpu.make_async_remote_copy(
                src_ref=buf.at[pl.ds(leaves, width)],
                dst_ref=buf.at[pl.ds(0, width)],
                send_sem=halo_send.at[2 * i],
                recv_sem=halo_recv.at[2 * i],
                device_id=right,
                device_id_type=MESH,
            )
        )
        to_left.append(
            pltpu.make_async_remote_copy(
                src_ref=buf.at[pl.ds(width, width)],
                dst_ref=buf.at[pl.ds(leaves + width, width)],
                send_sem=halo_send.at[2 * i + 1],
                recv_sem=halo_recv.at[2 * i + 1],
                device_id=left,
                device_id_type=MESH,
            )
        )
    for i in range(3):
        to_right[i].start()
        to_left[i].start()

    loads[3].wait()

    def nm_done(i, carry):
        peer = lax.rem(e + i, members)
        pltpu.make_async_remote_copy(
            src_ref=group_nm.at[peer],
            dst_ref=group_nm.at[peer],
            send_sem=nm_send.at[peer],
            recv_sem=nm_recv.at[peer],
            device_id=(g, peer),
            device_id_type=MESH,
        ).wait()
        return carry

    lax.fori_loop(1, members, nm_done, 0)
    top = jnp.zeros((group_nm.shape[1], rank), F)
    for i in range(members):
        top = top + dot_t(group_nm[i][:, :rank], lift_v[0, i])
    top_own[...] = twice(top).astype(BF)

    @pl.when(jnp.logical_and(is_catcher, kind == own_kind))
    def _():
        top_all[g // kinds] = top_own[...]


    def tm_copy(i):
        return pltpu.make_async_remote_copy(
            src_ref=top_own,
            dst_ref=top_all.at[g // kinds],
            send_sem=tm_send.at[i],
            recv_sem=tm_recv.at[g // kinds],
            device_id=(e * share + i, target_member),
            device_id_type=MESH,
        )

    for i in range(share):

        @pl.when(e * share + i != g)
        def _(i=i):
            tm_copy(i).start()

    pl.when(jnp.logical_not(ahead))(near_inner)
    for i in range(2):
        to_left[i].wait_recv()
    lax.fori_loop(NEAR + leaves, leaves + 2 * NEAR, sources, 0, unroll=4)
    lax.fori_loop(leaves - NEAR, leaves, near, 0, unroll=2)
    for i in range(2):
        to_right[i].wait_recv()
    lax.fori_loop(0, NEAR, sources, 0, unroll=4)
    lax.fori_loop(0, NEAR, near, 0, unroll=2)

    loads[4].wait()
    to_left[2].wait_recv()
    to_right[2].wait_recv()

    def couple(t, carry):
        m = []
        for j in range(far_list.shape[0]):
            s = lax.rem(far_list[j, t] - first + FAR + total, total)
            m.append(ext_mo[jnp.clip(s, 0, ext_mo.shape[0] - 1)])
        lhs = [pair(m[j], m[j + 1]) for j in range(0, len(m), 2)]
        coupled[t] = dot_t(jnp.concatenate(lhs, 1), coupling_v[t])
        return carry

    lax.fori_loop(0, leaves, couple, 0, unroll=8)
    loads[5].wait()
    nodes = pair(group_nm[node_list[0, 0]], group_nm[node_list[0, 1]])
    group_local = dot_t(nodes, ncoup_v[0])

    loads[6].wait()

    def part_copy(i):
        return pltpu.make_async_remote_copy(
            src_ref=top_part.at[kind],
            dst_ref=top_part.at[kind],
            send_sem=tl_send.at[i],
            recv_sem=tl_recv.at[kind],
            device_id=(g, lax.rem(e + i, members)),
            device_id_type=MESH,
        )

    @pl.when(is_catcher)
    def _():
        def tm_done(i, carry):
            peer = i * kinds + kind

            @pl.when(peer != g)
            def _():
                pltpu.make_async_remote_copy(
                    src_ref=top_all.at[i],
                    dst_ref=top_all.at[i],
                    send_sem=tm_send.at[0],
                    recv_sem=tm_recv.at[i],
                    device_id=(peer, g // share),
                    device_id_type=MESH,
                ).wait_recv()

            return carry

        lax.fori_loop(0, quarter, tm_done, 0)
        terms = []
        for j in range(top_list.shape[1]):
            source = top_list[0, j]
            here = jnp.where(lax.rem(source, kinds) == kind, F(1), F(0)).astype(BF)
            terms.append(top_all[jnp.clip(source // kinds, 0, quarter - 1)] * here)
        lhs = [pair(terms[j], terms[j + 1]) for j in range(0, len(terms), 2)]
        top_part[kind] = twice(dot_t(jnp.concatenate(lhs, 1), tcoup_v[0]))

        def part_start(i, carry):
            part_copy(i).start()
            return carry

        lax.fori_loop(1, members, part_start, 0)

    for k in range(kinds):

        @pl.when(catcher + k != e)
        def _(k=k):
            pltpu.make_async_remote_copy(
                src_ref=top_part.at[k],
                dst_ref=top_part.at[k],
                send_sem=tl_send.at[0],
                recv_sem=tl_recv.at[k],
                device_id=(g, catcher + k),
                device_id_type=MESH,
            ).wait_recv()

    top_local = jnp.sum(top_part[...], axis=0)[:, :rank].astype(BF)
    resident = group_local + jnp.dot(top_local, lift_v[0, e], preferred_element_type=F)
    wide = jnp.dot(resident.astype(BF), transfer_v[0], preferred_element_type=F)
    for u in range(leaves // 2):
        spread[u] = wide[:, 2 * rank * u : 2 * rank * (u + 1)]

    def finish(u, carry):
        base = spread[u]
        for h in range(2):
            t = 2 * u + h
            local = (coupled[t] + base[:, rank * h : rank * (h + 1)]).astype(BF)
            far = jnp.dot(local, basis_v[t], preferred_element_type=F)
            out[t] = (near_acc[t] + far).astype(out.dtype)
        return carry

    lax.fori_loop(0, leaves // 2, finish, 0, unroll=4)

    for h in to_right + to_left:
        h.wait_send()
    for i in range(share):

        @pl.when(e * share + i != g)
        def _(i=i):
            tm_copy(i).wait_send()

    @pl.when(is_catcher)
    def _():
        def part_sent(i, carry):
            part_copy(i).wait_send()
            return carry

        lax.fori_loop(1, members, part_sent, 0)


def shards(
    charges, points, near_list, near_count, basis, far_list, coupling, transfer, node_list,
    node_coupling, lift, top_list, top_coupling,
):
    leaves, right_sides, leaf_pts = charges.shape
    rank = basis.shape[1]
    members = lax.axis_size("grp")
    groups = lax.axis_size("leaf")
    share = groups // members
    kinds = 4
    smem = pl.BlockSpec(memory_space=pltpu.SMEM)
    vmem = pl.BlockSpec(memory_space=pltpu.VMEM)
    hbm = pl.BlockSpec(memory_space=pl.ANY)
    scratch = [
        pltpu.VMEM((leaves + 2 * NEAR, right_sides, leaf_pts), BF),
        pltpu.VMEM((leaves + 2 * NEAR, 16, leaf_pts), BF),
        pltpu.VMEM((leaves + 2 * FAR, right_sides, 2 * rank), BF),
        pltpu.VMEM((3, leaves, leaf_pts), F),
        pltpu.VMEM((leaves + 2 * NEAR, right_sides, leaf_pts), BF),
        pltpu.VMEM((leaves + 2 * NEAR, 3, 16, leaf_pts), BF),
        pltpu.VMEM((leaves, 3, leaf_pts, leaf_pts), BF),
        pltpu.VMEM((leaves, right_sides, leaf_pts), F),
        pltpu.VMEM((leaves // 2, right_sides, 2 * rank), F),
        pltpu.VMEM((leaves, right_sides, rank), F),
        pltpu.VMEM(basis.shape, BF),
        pltpu.VMEM(coupling.shape, BF),
        pltpu.VMEM(transfer.shape, BF),
        pltpu.VMEM(node_coupling.shape, BF),
        pltpu.VMEM(lift.shape, BF),
        pltpu.VMEM(top_coupling.shape, BF),
        pltpu.VMEM((members, right_sides, 2 * rank), BF),
        pltpu.VMEM((right_sides, 2 * rank), BF),
        pltpu.VMEM((groups // kinds, right_sides, 2 * rank), BF),
        pltpu.VMEM((kinds, right_sides, 2 * rank), F),
        pltpu.SemaphoreType.DMA((7,)),
        pltpu.SemaphoreType.DMA((6,)),
        pltpu.SemaphoreType.DMA((6,)),
        pltpu.SemaphoreType.DMA((members,)),
        pltpu.SemaphoreType.DMA((members,)),
        pltpu.SemaphoreType.DMA((share,)),
        pltpu.SemaphoreType.DMA((groups // kinds,)),
        pltpu.SemaphoreType.DMA((members,)),
        pltpu.SemaphoreType.DMA((kinds,)),
    ]
    result = pl.pallas_call(
        functools.partial(kernel, leaves * members * groups),
        out_shape=jax.ShapeDtypeStruct((leaves, right_sides, leaf_pts), F),
        in_specs=[smem] * 5 + [hbm, vmem] + [hbm] * 6,
        out_specs=vmem,
        scratch_shapes=scratch,
        compiler_params=pltpu.CompilerParams(
            collective_id=0, has_side_effects=True, vmem_limit_bytes=56 * 2**20
        ),
    )(
        near_list.T, near_count, far_list.T, node_list, top_list, charges, points.transpose(1, 0, 2), basis, coupling,
        transfer, node_coupling, lift, top_coupling,
    )
    return result.astype(BF)


def solution(mesh):
    both = ("leaf", "grp")
    return jax.shard_map(
        shards,
        mesh=mesh,
        in_specs=(
            P(both, None, None),
            P(both, None, None),
            P(both, None),
            P(both),
            P(both, None, None),
            P(both, None),
            P(both, None, None),
            P(both, None, None),
            P(both, None),
            P(both, None, None),
            P("leaf", None, None, None),
            P("leaf", None),
            P("leaf", None, None),
        ),
        out_specs=P(both, None, None),
        check_vma=False,
    )
```

time: 284 us -> 58.4 us (0.21)
  the two profiles are of different devices: /device:TPU:2 before, /device:TPU:344 now
where the time goes in v1:
time: 58.4 us; the launch traced here: 58.1 us
  Pallas kernels  56.5 us (97%)
  other arithmetic  1.62 us (3%)
    pallas_call x1, Pallas kernels, shards(): pl.pallas_call(functools.partial(kernel, leaves * members * groups), out_...  56.5 us
    convert_element_type x1, other arithmetic, shards(): return result.astype(BF)  1.62 us

profile of v1, /device:TPU:344, one launch (start us, length us, event | category | flops | bytes accessed | tf_op | source)
XLA Modules:
  0.0 58.1 jit_solution(16902601977167500868)
XLA Ops:
  0.0 56.5 %shard_map.127 = f32[32,16,128]{2,1,0:T(8,128)} custom-call(s32[20,32]{1,0:T(8,128)} %bitcast.4, s32[32]{0:T(128)} %near_count.1, s32[6,32]{1,0:T(8,128)} %bitcast.5, s32[1,2]{1,0:T(1,128)} %node_list.1, s32[1,4]{1,0:T(1,128)} %top_list.1, bf16[32,16,128]{2,1,0:T(8,128)(2,1)} %charges.1, bf16[3,32,128]{2,1,0:T(8,128)(2,1)} %bitcast.3, ...), custom_call_target="tpu_custom_call" | custom-call | tf_op jit(solution)/shard_map/pallas_call | solution.py:444
  56.5 1.6 %convert_element_type.3 = bf16[32,16,128]{2,1,0:T(8,128)(2,1)} convert(f32[32,16,128]{2,1,0:T(8,128)} %shard_map.127) | non-fusion elementwise | flops 65536 | bytes 393216 | tf_op jit(solution)/shard_map/convert_element_type | solution.py:457

commit v2 on v1

--- a/solution.py
+++ b/solution.py
@@ -9,7 +9,7 @@
 
 NEAR = 12
 FAR = 20
-EARLY = 6
+EARLY = 4
 BF = jnp.bfloat16
 F = jnp.float32
 MESH = pl.DeviceIdType.MESH
@@ -28,7 +28,7 @@
     total, near_list, near_count, far_list, node_list, top_list,
     charges, points, basis, coupling, transfer, node_coupling, lift, top_coupling,
     out,
-    ext_ch, ext_pt, ext_mo, fine, src_ch, rows, tiles, near_acc, spread, coupled,
+    ext_ch, ext_pt, ext_mo, fine, src_ch, rows, tiles, near_acc, spread, coupled, group_loc,
     basis_v, coupling_v, transfer_v, ncoup_v, lift_v, tcoup_v, group_nm, top_own, top_all, top_part,
     load_sem, halo_send, halo_recv, nm_send, nm_recv, tm_send, tm_recv, tl_send, tl_recv,
 ):
@@ -177,20 +177,15 @@
         near_acc[t] = acc * scale
         return carry
 
-    def near_inner():
-        lax.fori_loop(0, leaves, own_tiles, 0, unroll=2)
-        lax.fori_loop(0, NEAR, no_source, 0, unroll=4)
-        lax.fori_loop(NEAR + leaves, leaves + 2 * NEAR, no_source, 0, unroll=4)
-        lax.fori_loop(NEAR, NEAR + leaves, sources, 0, unroll=4)
-        lax.fori_loop(NEAR, leaves - NEAR, near, 0, unroll=2)
+    def near_pair(u, carry):
+        near(2 * u, carry)
+        return near(2 * u + 1, carry)
 
     ahead = lax.rem(g, groups // 2) < groups // EARLY
-    pl.when(ahead)(near_inner)
-
-    begin = e * share
-    mine = jnp.logical_and(g >= begin, g < begin + share)
-    targets = jnp.where(mine, share - 1, share)
-    pl.semaphore_wait(barrier, 2 + (members - 1) + targets)
+    lax.fori_loop(0, leaves, own_tiles, 0, unroll=2)
+    lax.fori_loop(0, NEAR, no_source, 0, unroll=4)
+    lax.fori_loop(NEAR + leaves, leaves + 2 * NEAR, no_source, 0, unroll=4)
+    lax.fori_loop(NEAR, NEAR + leaves, sources, 0, unroll=4)
 
     def nm_copy(i):
         peer = lax.rem(e + i, members)
@@ -202,12 +197,6 @@
             device_id=(g, peer),
             device_id_type=MESH,
         )
-
-    def nm_start(i, carry):
-        nm_copy(i).start()
-        return carry
-
-    lax.fori_loop(1, members, nm_start, 0)
 
     to_right = []
     to_left = []
@@ -232,35 +221,6 @@
                 device_id_type=MESH,
             )
         )
-    for i in range(3):
-        to_right[i].start()
-        to_left[i].start()
-
-    loads[3].wait()
-
-    def nm_done(i, carry):
-        peer = lax.rem(e + i, members)
-        pltpu.make_async_remote_copy(
-            src_ref=group_nm.at[peer],
-            dst_ref=group_nm.at[peer],
-            send_sem=nm_send.at[peer],
-            recv_sem=nm_recv.at[peer],
-            device_id=(g, peer),
-            device_id_type=MESH,
-        ).wait()
-        return carry
-
-    lax.fori_loop(1, members, nm_done, 0)
-    top = jnp.zeros((group_nm.shape[1], rank), F)
-    for i in range(members):
-        top = top + dot_t(group_nm[i][:, :rank], lift_v[0, i])
-    top_own[...] = twice(top).astype(BF)
-
-    @pl.when(jnp.logical_and(is_catcher, kind == own_kind))
-    def _():
-        top_all[g // kinds] = top_own[...]
-
-
     def tm_copy(i):
         return pltpu.make_async_remote_copy(
             src_ref=top_own,
@@ -271,42 +231,6 @@
             device_id_type=MESH,
         )
 
-    for i in range(share):
-
-        @pl.when(e * share + i != g)
-        def _(i=i):
-            tm_copy(i).start()
-
-    pl.when(jnp.logical_not(ahead))(near_inner)
-    for i in range(2):
-        to_left[i].wait_recv()
-    lax.fori_loop(NEAR + leaves, leaves + 2 * NEAR, sources, 0, unroll=4)
-    lax.fori_loop(leaves - NEAR, leaves, near, 0, unroll=2)
-    for i in range(2):
-        to_right[i].wait_recv()
-    lax.fori_loop(0, NEAR, sources, 0, unroll=4)
-    lax.fori_loop(0, NEAR, near, 0, unroll=2)
-
-    loads[4].wait()
-    to_left[2].wait_recv()
-    to_right[2].wait_recv()
-
-    def couple(t, carry):
-        m = []
-        for j in range(far_list.shape[0]):
-            s = lax.rem(far_list[j, t] - first + FAR + total, total)
-            m.append(ext_mo[jnp.clip(s, 0, ext_mo.shape[0] - 1)])
-        lhs = [pair(m[j], m[j + 1]) for j in range(0, len(m), 2)]
-        coupled[t] = dot_t(jnp.concatenate(lhs, 1), coupling_v[t])
-        return carry
-
-    lax.fori_loop(0, leaves, couple, 0, unroll=8)
-    loads[5].wait()
-    nodes = pair(group_nm[node_list[0, 0]], group_nm[node_list[0, 1]])
-    group_local = dot_t(nodes, ncoup_v[0])
-
-    loads[6].wait()
-
     def part_copy(i):
         return pltpu.make_async_remote_copy(
             src_ref=top_part.at[kind],
@@ -317,38 +241,141 @@
             device_id_type=MESH,
         )
 
-    @pl.when(is_catcher)
-    def _():
-        def tm_done(i, carry):
-            peer = i * kinds + kind
-
-            @pl.when(peer != g)
-            def _():
-                pltpu.make_async_remote_copy(
-                    src_ref=top_all.at[i],
-                    dst_ref=top_all.at[i],
-                    send_sem=tm_send.at[0],
-                    recv_sem=tm_recv.at[i],
-                    device_id=(peer, g // share),
-                    device_id_type=MESH,
-                ).wait_recv()
-
+    def enter():
+        begin = e * share
+        mine = jnp.logical_and(g >= begin, g < begin + share)
+        targets = jnp.where(mine, share - 1, share)
+        pl.semaphore_wait(barrier, 2 + (members - 1) + targets)
+
+        def nm_start(i, carry):
+            nm_copy(i).start()
             return carry
 
-        lax.fori_loop(0, quarter, tm_done, 0)
-        terms = []
-        for j in range(top_list.shape[1]):
-            source = top_list[0, j]
-            here = jnp.where(lax.rem(source, kinds) == kind, F(1), F(0)).astype(BF)
-            terms.append(top_all[jnp.clip(source // kinds, 0, quarter - 1)] * here)
-        lhs = [pair(terms[j], terms[j + 1]) for j in range(0, len(terms), 2)]
-        top_part[kind] = twice(dot_t(jnp.concatenate(lhs, 1), tcoup_v[0]))
-
-        def part_start(i, carry):
-            part_copy(i).start()
+        lax.fori_loop(1, members, nm_start, 0)
+
+        for i in range(3):
+            to_right[i].start()
+            to_left[i].start()
+
+    def lift_group():
+        loads[3].wait()
+
+        def nm_done(i, carry):
+            peer = lax.rem(e + i, members)
+            pltpu.make_async_remote_copy(
+                src_ref=group_nm.at[peer],
+                dst_ref=group_nm.at[peer],
+                send_sem=nm_send.at[peer],
+                recv_sem=nm_recv.at[peer],
+                device_id=(g, peer),
+                device_id_type=MESH,
+            ).wait()
             return carry
 
-        lax.fori_loop(1, members, part_start, 0)
+        lax.fori_loop(1, members, nm_done, 0)
+        top = jnp.zeros((group_nm.shape[1], rank), F)
+        for i in range(members):
+            top = top + dot_t(group_nm[i][:, :rank], lift_v[0, i])
+        top_own[...] = twice(top).astype(BF)
+
+        @pl.when(jnp.logical_and(is_catcher, kind == own_kind))
+        def _():
+            top_all[g // kinds] = top_own[...]
+
+
+        for i in range(share):
+
+            @pl.when(e * share + i != g)
+            def _(i=i):
+                tm_copy(i).start()
+
+    def from_right():
+        for i in range(2):
+            to_left[i].wait_recv()
+        lax.fori_loop(NEAR + leaves, leaves + 2 * NEAR, sources, 0, unroll=4)
+
+    def hand_on():
+        loads[4].wait()
+        to_left[2].wait_recv()
+        to_right[2].wait_recv()
+
+        def couple(t, carry):
+            m = []
+            for j in range(far_list.shape[0]):
+                s = lax.rem(far_list[j, t] - first + FAR + total, total)
+                m.append(ext_mo[jnp.clip(s, 0, ext_mo.shape[0] - 1)])
+            lhs = [pair(m[j], m[j + 1]) for j in range(0, len(m), 2)]
+            coupled[t] = dot_t(jnp.concatenate(lhs, 1), coupling_v[t])
+            return carry
+
+        lax.fori_loop(0, leaves, couple, 0, unroll=8)
+        loads[5].wait()
+        nodes = pair(group_nm[node_list[0, 0]], group_nm[node_list[0, 1]])
+        group_loc[...] = dot_t(nodes, ncoup_v[0])
+
+        loads[6].wait()
+
+        @pl.when(is_catcher)
+        def _():
+            def tm_done(i, carry):
+                peer = i * kinds + kind
+
+                @pl.when(peer != g)
+                def _():
+                    pltpu.make_async_remote_copy(
+                        src_ref=top_all.at[i],
+                        dst_ref=top_all.at[i],
+                        send_sem=tm_send.at[0],
+                        recv_sem=tm_recv.at[i],
+                        device_id=(peer, g // share),
+                        device_id_type=MESH,
+                    ).wait_recv()
+
+                return carry
+
+            lax.fori_loop(0, quarter, tm_done, 0)
+            terms = []
+            for j in range(top_list.shape[1]):
+                source = top_list[0, j]
+                here = jnp.where(lax.rem(source, kinds) == kind, F(1), F(0)).astype(BF)
+                terms.append(top_all[jnp.clip(source // kinds, 0, quarter - 1)] * here)
+            lhs = [pair(terms[j], terms[j + 1]) for j in range(0, len(terms), 2)]
+            top_part[kind] = twice(dot_t(jnp.concatenate(lhs, 1), tcoup_v[0]))
+
+            def part_start(i, carry):
+                part_copy(i).start()
+                return carry
+
+            lax.fori_loop(1, members, part_start, 0)
+
+        for i in range(2):
+            to_right[i].wait_recv()
+        lax.fori_loop(0, NEAR, sources, 0, unroll=4)
+
+    edge = NEAR // 2
+    inner = leaves // 2 - 2 * edge
+    half = inner // 2
+    free = jnp.where(ahead, inner, 0)
+    steps = [
+        (None, edge, free),
+        (enter, edge, jnp.where(ahead, 0, half)),
+        (lift_group, edge + half, jnp.where(ahead, 0, inner - half)),
+        (from_right, edge + inner, edge),
+        (hand_on, 0, edge),
+    ]
+
+    def phase(p, carry):
+        begin = 0
+        size = 0
+        for i, (step, start, count) in enumerate(steps):
+            if step is not None:
+                pl.when(p == i)(step)
+            begin = jnp.where(p == i, start, begin)
+            size = jnp.where(p == i, count, size)
+        lax.fori_loop(begin, begin + size, near_pair, 0)
+        return carry
+
+    lax.fori_loop(0, len(steps), phase, 0)
 
     for k in range(kinds):
 
@@ -364,7 +391,7 @@
             ).wait_recv()
 
     top_local = jnp.sum(top_part[...], axis=0)[:, :rank].astype(BF)
-    resident = group_local + jnp.dot(top_local, lift_v[0, e], preferred_element_type=F)
+    resident = group_loc[...] + jnp.dot(top_local, lift_v[0, e], preferred_element_type=F)
     wide = jnp.dot(resident.astype(BF), transfer_v[0], preferred_element_type=F)
     for u in range(leaves // 2):
         spread[u] = wide[:, 2 * rank * u : 2 * rank * (u + 1)]
@@ -421,6 +448,7 @@
         pltpu.VMEM((leaves, right_sides, leaf_pts), F),
         pltpu.VMEM((leaves // 2, right_sides, 2 * rank), F),
         pltpu.VMEM((leaves, right_sides, rank), F),
+        pltpu.VMEM((right_sides, rank), F),
         pltpu.VMEM(basis.shape, BF),
         pltpu.VMEM(coupling.shape, BF),
         pltpu.VMEM(transfer.shape, BF),

time: 58.4 us -> 53 us (0.908)
  the two profiles are of different devices: /device:TPU:344 before, /device:TPU:5 now
where the time goes in v2:
time: 53 us; the launch traced here: 52.8 us
  Pallas kernels  51.1 us (96%)
  other arithmetic  1.62 us (3%)
    pallas_call x1, Pallas kernels, shards(): pl.pallas_call(functools.partial(kernel, leaves * members * groups), out_...  51.1 us
    convert_element_type x1, other arithmetic, shards(): return result.astype(BF)  1.62 us

profile of v2, /device:TPU:5, one launch (start us, length us, event | category | flops | bytes accessed | tf_op | source)
XLA Modules:
  0.0 52.8 jit_solution(12933946651467172430)
XLA Ops:
  0.0 51.1 %shard_map.127 = f32[32,16,128]{2,1,0:T(8,128)} custom-call(s32[20,32]{1,0:T(8,128)} %bitcast.4, s32[32]{0:T(128)} %near_count.1, s32[6,32]{1,0:T(8,128)} %bitcast.5, s32[1,2]{1,0:T(1,128)} %node_list.1, s32[1,4]{1,0:T(1,128)} %top_list.1, bf16[32,16,128]{2,1,0:T(8,128)(2,1)} %charges.1, bf16[3,32,128]{2,1,0:T(8,128)(2,1)} %bitcast.3, ...), custom_call_target="tpu_custom_call" | custom-call | tf_op jit(solution)/shard_map/pallas_call | solution.py:472
  51.2 1.6 %convert_element_type.3 = bf16[32,16,128]{2,1,0:T(8,128)(2,1)} convert(f32[32,16,128]{2,1,0:T(8,128)} %shard_map.127) | non-fusion elementwise | flops 65536 | bytes 393216 | tf_op jit(solution)/shard_map/convert_element_type | solution.py:485

commit v3 on v2

--- a/solution.py
+++ b/solution.py
@@ -182,10 +182,13 @@
         return near(2 * u + 1, carry)
 
     ahead = lax.rem(g, groups // 2) < groups // EARLY
-    lax.fori_loop(0, leaves, own_tiles, 0, unroll=2)
-    lax.fori_loop(0, NEAR, no_source, 0, unroll=4)
-    lax.fori_loop(NEAR + leaves, leaves + 2 * NEAR, no_source, 0, unroll=4)
-    lax.fori_loop(NEAR, NEAR + leaves, sources, 0, unroll=4)
+    def prepare_tiles():
+        lax.fori_loop(0, leaves, own_tiles, 0, unroll=2)
+
+    def prepare_sources():
+        lax.fori_loop(0, NEAR, no_source, 0, unroll=4)
+        lax.fori_loop(NEAR + leaves, leaves + 2 * NEAR, no_source, 0, unroll=4)
+        lax.fori_loop(NEAR, NEAR + leaves, sources, 0, unroll=4)
 
     def nm_copy(i):
         peer = lax.rem(e + i, members)
@@ -348,34 +351,46 @@
 
             lax.fori_loop(1, members, part_start, 0)
 
+    def from_left():
         for i in range(2):
             to_right[i].wait_recv()
         lax.fori_loop(0, NEAR, sources, 0, unroll=4)
 
     edge = NEAR // 2
     inner = leaves // 2 - 2 * edge
-    half = inner // 2
-    free = jnp.where(ahead, inner, 0)
-    steps = [
-        (None, edge, free),
-        (enter, edge, jnp.where(ahead, 0, half)),
-        (lift_group, edge + half, jnp.where(ahead, 0, inner - half)),
-        (from_right, edge + inner, edge),
-        (hand_on, 0, edge),
+    late = jnp.logical_not(ahead)
+    phases = [
+        ([(prepare_tiles, ahead), (prepare_sources, ahead)], edge, jnp.where(ahead, inner, 0)),
+        ([(enter, None), (prepare_tiles, late)], edge, 0),
+        ([(lift_group, late), (prepare_sources, late)], edge, jnp.where(ahead, 0, inner)),
+        ([(from_right, None)], edge + inner, edge),
+        ([(lift_group, ahead), (from_left, None)], 0, edge // 2),
+        ([(hand_on, None)], edge // 2, edge - edge // 2),
     ]
 
     def phase(p, carry):
+        def run(step):
+            now = jnp.bool_(False)
+            for i, (steps, _, _) in enumerate(phases):
+                for other, when in steps:
+                    if other is step:
+                        here = p == i
+                        if when is not None:
+                            here = jnp.logical_and(here, when)
+                        now = jnp.logical_or(now, here)
+            pl.when(now)(step)
+
+        for step in (enter, prepare_tiles, lift_group, prepare_sources, from_right, from_left, hand_on):
+            run(step)
         begin = 0
         size = 0
-        for i, (step, start, count) in enumerate(steps):
-            if step is not None:
-                pl.when(p == i)(step)
+        for i, (_, start, count) in enumerate(phases):
             begin = jnp.where(p == i, start, begin)
             size = jnp.where(p == i, count, size)
         lax.fori_loop(begin, begin + size, near_pair, 0)
         return carry
 
-    lax.fori_loop(0, len(steps), phase, 0)
+    lax.fori_loop(0, len(phases), phase, 0)
 
     for k in range(kinds):
 
@@ -405,7 +420,7 @@
             out[t] = (near_acc[t] + far).astype(out.dtype)
         return carry
 
-    lax.fori_loop(0, leaves // 2, finish, 0, unroll=4)
+    lax.fori_loop(0, leaves // 2, finish, 0, unroll=8)
 
     for h in to_right + to_left:
         h.wait_send()
@@ -471,7 +486,7 @@
     ]
     result = pl.pallas_call(
         functools.partial(kernel, leaves * members * groups),
-        out_shape=jax.ShapeDtypeStruct((leaves, right_sides, leaf_pts), F),
+        out_shape=jax.ShapeDtypeStruct((leaves, right_sides, leaf_pts), BF),
         in_specs=[smem] * 5 + [hbm, vmem] + [hbm] * 6,
         out_specs=vmem,
         scratch_shapes=scratch,
@@ -482,7 +497,7 @@
         near_list.T, near_count, far_list.T, node_list, top_list, charges, points.transpose(1, 0, 2), basis, coupling,
         transfer, node_coupling, lift, top_coupling,
     )
-    return result.astype(BF)
+    return result
 
 
 def solution(mesh):

time: 53 us -> 56.8 us (1.072)
  the two profiles are of different devices: /device:TPU:5 before, /device:TPU:24 now
where the time goes in v3:
time: 56.8 us; the launch traced here: 56.5 us
  Pallas kernels  55 us (97%)
  local copies, waits for them, and re-layouts  1.57 us (3%)
    pallas_call x1, Pallas kernels, shards(): pl.pallas_call(functools.partial(kernel, leaves * members * groups), out_...  55 us
    unnamed x1, local copies, waits for them, and re-layouts  1.57 us

profile of v3, /device:TPU:24, one launch (start us, length us, event | category | flops | bytes accessed | tf_op | source)
XLA Modules:
  0.0 56.5 jit_solution(11945225906975357681)
XLA Ops:
  0.0 55.0 %shard_map.127 = bf16[32,16,128]{2,1,0:T(8,128)(2,1)} custom-call(s32[20,32]{1,0:T(8,128)} %bitcast.4, s32[32]{0:T(128)} %near_count.1, s32[6,32]{1,0:T(8,128)} %bitcast.5, s32[1,2]{1,0:T(1,128)} %node_list.1, s32[1,4]{1,0:T(1,128)} %top_list.1, bf16[32,16,128]{2,1,0:T(8,128)(2,1)} %charges.1, bf16[3,32,128]{2,1,0:T(8,128)(2,1)} %bitcast.3, ...), custom_call_target="tpu_custom_call" | custom-call | tf_op jit(solution)/shard_map/pallas_call | solution.py:487
  55.0 1.6 %copy.15 = bf16[32,16,128]{2,1,0:T(8,128)(2,1)} copy(bf16[32,16,128]{2,1,0:T(8,128)(2,1)} %shard_map.127) | data formatting | bytes 262144

commit v4 on v2

--- a/solution.py
+++ b/solution.py
@@ -177,9 +177,10 @@
         near_acc[t] = acc * scale
         return carry
 
-    def near_pair(u, carry):
-        near(2 * u, carry)
-        return near(2 * u + 1, carry)
+    def near_four(u, carry):
+        for i in range(4):
+            near(4 * u + i, carry)
+        return carry
 
     ahead = lax.rem(g, groups // 2) < groups // EARLY
     lax.fori_loop(0, leaves, own_tiles, 0, unroll=2)
@@ -352,30 +353,43 @@
             to_right[i].wait_recv()
         lax.fori_loop(0, NEAR, sources, 0, unroll=4)
 
-    edge = NEAR // 2
-    inner = leaves // 2 - 2 * edge
+    edge = NEAR // 4
+    inner = leaves // 4 - 2 * edge
     half = inner // 2
-    free = jnp.where(ahead, inner, 0)
-    steps = [
-        (None, edge, free),
-        (enter, edge, jnp.where(ahead, 0, half)),
-        (lift_group, edge + half, jnp.where(ahead, 0, inner - half)),
-        (from_right, edge + inner, edge),
-        (hand_on, 0, edge),
+    late = jnp.logical_not(ahead)
+
+    def choose(a, b):
+        return jnp.where(ahead, a, b)
+
+    phases = [
+        ([], edge, choose(inner, 0)),
+        ([(enter, True), (from_right, ahead)], choose(edge + inner, edge), choose(1, half)),
+        (
+            [(lift_group, True)],
+            choose(edge + inner + 1, edge + half),
+            choose(edge - 1, inner - half),
+        ),
+        ([(from_right, late)], edge + inner, choose(0, edge)),
+        ([(hand_on, True)], 0, edge),
     ]
 
     def phase(p, carry):
+        for step in (enter, lift_group, from_right, hand_on):
+            now = False
+            for i, (steps, _, _) in enumerate(phases):
+                for other, takes in steps:
+                    if other is step:
+                        now = jnp.logical_or(now, jnp.logical_and(p == i, takes))
+            pl.when(now)(step)
         begin = 0
         size = 0
-        for i, (step, start, count) in enumerate(steps):
-            if step is not None:
-                pl.when(p == i)(step)
+        for i, (_, start, count) in enumerate(phases):
             begin = jnp.where(p == i, start, begin)
             size = jnp.where(p == i, count, size)
-        lax.fori_loop(begin, begin + size, near_pair, 0)
-        return carry
-
-    lax.fori_loop(0, len(steps), phase, 0)
+        lax.fori_loop(begin, begin + size, near_four, 0)
+        return carry
+
+    lax.fori_loop(0, len(phases), phase, 0)
 
     for k in range(kinds):
 
@@ -405,7 +419,7 @@
             out[t] = (near_acc[t] + far).astype(out.dtype)
         return carry
 
-    lax.fori_loop(0, leaves // 2, finish, 0, unroll=4)
+    lax.fori_loop(0, leaves // 2, finish, 0, unroll=8)
 
     for h in to_right + to_left:
         h.wait_send()
@@ -471,7 +485,7 @@
     ]
     result = pl.pallas_call(
         functools.partial(kernel, leaves * members * groups),
-        out_shape=jax.ShapeDtypeStruct((leaves, right_sides, leaf_pts), F),
+        out_shape=jax.ShapeDtypeStruct((leaves, right_sides, leaf_pts), BF),
         in_specs=[smem] * 5 + [hbm, vmem] + [hbm] * 6,
         out_specs=vmem,
         scratch_shapes=scratch,
@@ -482,7 +496,7 @@
         near_list.T, near_count, far_list.T, node_list, top_list, charges, points.transpose(1, 0, 2), basis, coupling,
         transfer, node_coupling, lift, top_coupling,
     )
-    return result.astype(BF)
+    return result
 
 
 def solution(mesh):

time: 53 us -> 53.3 us (level)
  other arithmetic: 1.62 us -> 0 us
  local copies, waits for them, and re-layouts: 0 us -> 1.57 us
    convert_element_type x1 -> x0, other arithmetic: 1.62 us -> none  [shards(): return result.astype(BF)]
    unnamed x0 -> x1, local copies, waits for them, and re-layouts: none -> 1.57 us
where the time goes in v4:
time: 53.3 us; the launch traced here: 53 us
  Pallas kernels  51.4 us (96%)
  local copies, waits for them, and re-layouts  1.57 us (3%)
    pallas_call x1, Pallas kernels, shards(): pl.pallas_call(functools.partial(kernel, leaves * members * groups), out_...  51.4 us
    unnamed x1, local copies, waits for them, and re-layouts  1.57 us

profile of v4, /device:TPU:5, one launch (start us, length us, event | category | flops | bytes accessed | tf_op | source)
XLA Modules:
  0.0 53.0 jit_solution(3076574667790620540)
XLA Ops:
  0.0 51.4 %shard_map.127 = bf16[32,16,128]{2,1,0:T(8,128)(2,1)} custom-call(s32[20,32]{1,0:T(8,128)} %bitcast.4, s32[32]{0:T(128)} %near_count.1, s32[6,32]{1,0:T(8,128)} %bitcast.5, s32[1,2]{1,0:T(1,128)} %node_list.1, s32[1,4]{1,0:T(1,128)} %top_list.1, bf16[32,16,128]{2,1,0:T(8,128)(2,1)} %charges.1, bf16[3,32,128]{2,1,0:T(8,128)(2,1)} %bitcast.3, ...), custom_call_target="tpu_custom_call" | custom-call | tf_op jit(solution)/shard_map/pallas_call | solution.py:486
  51.4 1.6 %copy.15 = bf16[32,16,128]{2,1,0:T(8,128)(2,1)} copy(bf16[32,16,128]{2,1,0:T(8,128)(2,1)} %shard_map.127) | data formatting | bytes 262144

commit v5 on v4

--- a/solution.py
+++ b/solution.py
@@ -184,9 +184,11 @@
 
     ahead = lax.rem(g, groups // 2) < groups // EARLY
     lax.fori_loop(0, leaves, own_tiles, 0, unroll=2)
-    lax.fori_loop(0, NEAR, no_source, 0, unroll=4)
-    lax.fori_loop(NEAR + leaves, leaves + 2 * NEAR, no_source, 0, unroll=4)
-    lax.fori_loop(NEAR, NEAR + leaves, sources, 0, unroll=4)
+
+    def own_sources():
+        lax.fori_loop(0, NEAR, no_source, 0, unroll=4)
+        lax.fori_loop(NEAR + leaves, leaves + 2 * NEAR, no_source, 0, unroll=4)
+        lax.fori_loop(NEAR, NEAR + leaves, sources, 0, unroll=4)
 
     def nm_copy(i):
         peer = lax.rem(e + i, members)
@@ -349,6 +351,7 @@
 
             lax.fori_loop(1, members, part_start, 0)
 
+    def from_left():
         for i in range(2):
             to_right[i].wait_recv()
         lax.fori_loop(0, NEAR, sources, 0, unroll=4)
@@ -362,19 +365,20 @@
         return jnp.where(ahead, a, b)
 
     phases = [
-        ([], edge, choose(inner, 0)),
-        ([(enter, True), (from_right, ahead)], choose(edge + inner, edge), choose(1, half)),
+        ([(own_sources, ahead)], edge, choose(inner, 0)),
+        ([(enter, True), (own_sources, late), (from_right, ahead)], choose(edge + inner, edge), choose(1, half)),
         (
             [(lift_group, True)],
             choose(edge + inner + 1, edge + half),
             choose(edge - 1, inner - half),
         ),
         ([(from_right, late)], edge + inner, choose(0, edge)),
-        ([(hand_on, True)], 0, edge),
+        ([(from_left, True)], 0, 1),
+        ([(hand_on, True)], 1, edge - 1),
     ]
 
     def phase(p, carry):
-        for step in (enter, lift_group, from_right, hand_on):
+        for step in (enter, own_sources, lift_group, from_right, from_left, hand_on):
             now = False
             for i, (steps, _, _) in enumerate(phases):
                 for other, takes in steps:

time: 53.3 us -> 51.8 us (0.972)
  the two profiles are of different devices: /device:TPU:5 before, /device:TPU:24 now
where the time goes in v5:
time: 51.8 us; the launch traced here: 51.5 us
  Pallas kernels  50 us (97%)
  local copies, waits for them, and re-layouts  1.57 us (3%)
    pallas_call x1, Pallas kernels, shards(): pl.pallas_call(functools.partial(kernel, leaves * members * groups), out_...  50 us
    unnamed x1, local copies, waits for them, and re-layouts  1.57 us

profile of v5, /device:TPU:24, one launch (start us, length us, event | category | flops | bytes accessed | tf_op | source)
XLA Modules:
  0.0 51.5 jit_solution(9315282380459486921)
XLA Ops:
  0.0 50.0 %shard_map.127 = bf16[32,16,128]{2,1,0:T(8,128)(2,1)} custom-call(s32[20,32]{1,0:T(8,128)} %bitcast.4, s32[32]{0:T(128)} %near_count.1, s32[6,32]{1,0:T(8,128)} %bitcast.5, s32[1,2]{1,0:T(1,128)} %node_list.1, s32[1,4]{1,0:T(1,128)} %top_list.1, bf16[32,16,128]{2,1,0:T(8,128)(2,1)} %charges.1, bf16[3,32,128]{2,1,0:T(8,128)(2,1)} %bitcast.3, ...), custom_call_target="tpu_custom_call" | custom-call | tf_op jit(solution)/shard_map/pallas_call | solution.py:490
  50.0 1.6 %copy.15 = bf16[32,16,128]{2,1,0:T(8,128)(2,1)} copy(bf16[32,16,128]{2,1,0:T(8,128)(2,1)} %shard_map.127) | data formatting | bytes 262144
